TPU v7x, 32 devices: a whole 2x2x4 slice. The times are simulated.
32 devices in a mesh: dp: 8 (over z, core), seq: 4 (over y, x).
Axes of the slice: x: 2, y: 2, z: 4, core: 2. Of those that a mesh axis runs over, the one named last changes fastest.
Arguments:
- queries: bfloat16 [8, 1024, 1024], P('dp', 'seq'), may hold values from -80 to 80
- keys: bfloat16 [8, 1024, 1024], P('dp', 'seq'), may hold values from -80 to 80
- values: bfloat16 [8, 1024, 1024], P('dp', 'seq'), may hold values from -12 to 12
- upstream: bfloat16 [8, 1024, 1024], P('dp', 'seq'), may hold values from -6 to 6
- w_out: bfloat16 [1024, 1024], replicated, may hold values from -0.1875 to 0.1875
- key_blocks: int32 [8, 8, 4], P('dp'), may hold values from 0 to 7, as said below
- block_counts: int32 [8, 8], P('dp'), may hold values from 1 to 4, as said below
Outputs:
- mixed: bfloat16 [8, 1024, 1024], P('dp', 'seq')
- grad_q: bfloat16 [8, 1024, 1024], P('dp', 'seq')
- grad_k: bfloat16 [8, 1024, 1024], P('dp', 'seq')
- grad_v: bfloat16 [8, 1024, 1024], P('dp', 'seq')
- grad_wo: float32 [1024, 1024], P('seq', 'dp')
Inputs may be any that keep to these rules, and one draw needn't show every extreme that they name: `key_blocks`: row b of a sequence's lists holds 4 distinct block numbers, the first of them b itself; entries past block_counts are valid numbers and are not used. `block_counts`: every sequence has a query block with exactly 4 used entries.
All inputs are finite; a program needn't handle non-finite values.
Results may differ from a plain program's by a relative error of at most 0.039.
Values may be sent and summed in bfloat16 or wider, within the bound.
A program may use at most 128 MiB of HBM per device.

v0:
```python
import math

import jax
import jax.numpy as jnp
from jax import lax
from jax.sharding import PartitionSpec as P

HEADS = 16


blocks_per_step = 4


def product(form, left, right):
    return jnp.einsum(form, left, right, preferred_element_type=jnp.float32)


def inner_rows(left, right):
    return lax.dot_general(
        left, right, (((0,), (0,)), ((), ())), preferred_element_type=jnp.float32
    )


def block_attention(head_q, head_k, head_v, head_g, key_lists, key_counts):
    node_count, head_count, head_width = head_q.shape
    block_count, listed = key_lists.shape
    block_rows = node_count // block_count
    steps_count = block_count // blocks_per_step
    score_scale = 1.0 / math.sqrt(head_width)
    query_groups = head_q.reshape(steps_count, blocks_per_step, block_rows, head_count, head_width)
    grad_groups = head_g.reshape(steps_count, blocks_per_step, block_rows, head_count, head_width)
    key_table = head_k.reshape(block_count, block_rows, head_count, head_width)
    value_table = head_v.reshape(block_count, block_rows, head_count, head_width)
    list_groups = key_lists.reshape(steps_count, blocks_per_step, listed)
    count_groups = key_counts.reshape(steps_count, blocks_per_step)
    slot_index = jnp.arange(listed, dtype=jnp.int32)

    def one_step(accumulated, inputs):
        key_acc, value_acc = accumulated
        query_part, grad_part, list_part, count_part = inputs
        keys_near = key_table[list_part]
        values_near = value_table[list_part]
        scores = product("gqnd,gjknd->gnqjk", query_part, keys_near) * score_scale
        usable = (slot_index[None, :] < count_part[:, None])[:, None, None, :, None]
        scores = jnp.where(usable, scores, -jnp.inf)
        highest = jnp.max(scores, axis=(3, 4), keepdims=True)
        raised = jnp.exp(scores - highest)
        probability = raised / jnp.sum(raised, axis=(3, 4), keepdims=True)
        weights = probability.astype(jnp.bfloat16)
        attended = product("gnqjk,gjknd->gqnd", weights, values_near).astype(jnp.bfloat16)
        row_delta = jnp.sum(grad_part.astype(jnp.float32) * attended.astype(jnp.float32), axis=3)
        grad_scores = product("gqnd,gjknd->gnqjk", grad_part, values_near)
        shifted = grad_scores - jnp.transpose(row_delta, (0, 2, 1))[:, :, :, None, None]
        grad_logits = (probability * shifted).astype(jnp.bfloat16)
        grad_query = (product("gnqjk,gjknd->gqnd", grad_logits, keys_near) * score_scale).astype(
            jnp.bfloat16
        )
        key_terms = product("gnqjk,gqnd->gjknd", grad_logits, query_part) * score_scale
        value_terms = product("gnqjk,gqnd->gjknd", weights, grad_part)
        flat_list = list_part.reshape(-1)
        key_acc = key_acc.at[flat_list].add(
            key_terms.reshape(-1, block_rows, head_count, head_width)
        )
        value_acc = value_acc.at[flat_list].add(
            value_terms.reshape(-1, block_rows, head_count, head_width)
        )
        return ((key_acc, value_acc), (attended, grad_query))

    empty = jnp.zeros((block_count, block_rows, head_count, head_width), jnp.float32)
    (key_acc, value_acc), (attended, grad_query) = lax.scan(
        one_step, (empty, empty), (query_groups, grad_groups, list_groups, count_groups)
    )
    shape = (node_count, head_count, head_width)
    return (
        attended.reshape(shape),
        grad_query.reshape(shape),
        key_acc.astype(jnp.bfloat16).reshape(shape),
        value_acc.astype(jnp.bfloat16).reshape(shape),
    )


def project_back(up_rows, w_out):
    return lax.dot_general(
        up_rows, w_out, (((1,), (1,)), ((), ())), preferred_element_type=jnp.float32
    ).astype(jnp.bfloat16)


def local(queries, keys, values, upstream, w_out, key_blocks, block_counts):
    local_rows = queries.shape[1]
    width = queries.shape[2]
    head_width = width // HEADS
    up_rows = upstream[0]

    def split_heads(array):
        return array.reshape(local_rows, HEADS, head_width)

    query_heads = split_heads(queries[0])
    key_heads = split_heads(keys[0])
    value_heads = split_heads(values[0])
    grad_att = project_back(up_rows, w_out)
    head_q, head_k, head_v, head_g = (
        lax.all_to_all(query_heads, "seq", split_axis=1, concat_axis=0, tiled=True),
        lax.all_to_all(key_heads, "seq", split_axis=1, concat_axis=0, tiled=True),
        lax.all_to_all(value_heads, "seq", split_axis=1, concat_axis=0, tiled=True),
        lax.all_to_all(split_heads(grad_att), "seq", split_axis=1, concat_axis=0, tiled=True),
    )
    attended, grad_query, grad_key, grad_value = block_attention(
        head_q, head_k, head_v, head_g, key_blocks[0], block_counts[0]
    )
    node_att, node_gq, node_gk, node_gv = (
        lax.all_to_all(attended, "seq", split_axis=0, concat_axis=1, tiled=True),
        lax.all_to_all(grad_query, "seq", split_axis=0, concat_axis=1, tiled=True),
        lax.all_to_all(grad_key, "seq", split_axis=0, concat_axis=1, tiled=True),
        lax.all_to_all(grad_value, "seq", split_axis=0, concat_axis=1, tiled=True),
    )
    att_nodes = node_att.reshape(local_rows, width)
    mixed = jnp.dot(att_nodes, w_out, preferred_element_type=jnp.float32).astype(jnp.bfloat16)
    factor = 1.0 / math.sqrt(lax.axis_size("dp") * lax.axis_size("seq") * local_rows)
    summed = lax.psum_scatter(
        inner_rows(att_nodes, up_rows), "seq", scatter_dimension=0, tiled=True
    )
    grad_wo = lax.psum_scatter(summed, "dp", scatter_dimension=1, tiled=True)
    full_shape = (1, local_rows, width)
    return (
        mixed.reshape(full_shape),
        node_gq.reshape(full_shape),
        node_gk.reshape(full_shape),
        node_gv.reshape(full_shape),
        grad_wo * factor,
    )


def solution(mesh):
    placed = (
        P("dp", "seq", None),
        P("dp", "seq", None),
        P("dp", "seq", None),
        P("dp", "seq", None),
        P(),
        P("dp", None, None),
        P("dp", None),
    )
    return jax.shard_map(
        local,
        mesh=mesh,
        in_specs=placed,
        out_specs=(
            P("dp", "seq", None),
            P("dp", "seq", None),
            P("dp", "seq", None),
            P("dp", "seq", None),
            P("seq", "dp"),
        ),
        check_vma=False,
    )
```

profile of v0, /device:TPU:0, one launch (start us, length us, event | category | flops | bytes accessed | tf_op | source)
XLA Modules:
  0.0 285.2 jit_solution(2296870080193914179)
XLA Ops:
  7.2 2.2 copy.140
  9.4 5.2 %all-to-all-start = ((bf16[256,16,64]{0,2,1:T(8,128)(2,1)}), bf16[256,16,64]{0,2,1:T(8,128)(2,1)S(1)}, u32[]{:S(2)}, u32[]{:S(2)}) async-start(bf16[256,16,64]{0,2,1:T(8,128)(2,1)} %bitcast.1), calls=%async_computation | async-start | bytes 1048576 | tf_op jit(solution)/shard_map/all_to_all | solution.py:102
  14.6 2.0 copy.142
  16.6 6.0 %all-to-all-done = bf16[256,16,64]{0,2,1:T(8,128)(2,1)S(1)} async-done(((bf16[256,16,64]{0,2,1:T(8,128)(2,1)}), bf16[256,16,64]{0,2,1:T(8,128)(2,1)S(1)}, u32[]{:S(2)}, u32[]{:S(2)}) %all-to-all-start) | async-done | bytes 524320 | tf_op jit(solution)/shard_map/all_to_all | solution.py:102
  23.4 3.5 %all-to-all-start.1 = ((bf16[256,16,64]{0,2,1:T(8,128)(2,1)}), bf16[256,16,64]{0,2,1:T(8,128)(2,1)S(1)}, u32[]{:S(2)}, u32[]{:S(2)}) async-start(bf16[256,16,64]{0,2,1:T(8,128)(2,1)} %bitcast.4), calls=%async_computation.1 | async-start | bytes 1048576 | tf_op jit(solution)/shard_map/all_to_all | solution.py:103
  27.9 6.1 %all-to-all-done.1 = bf16[256,16,64]{0,2,1:T(8,128)(2,1)S(1)} async-done(((bf16[256,16,64]{0,2,1:T(8,128)(2,1)}), bf16[256,16,64]{0,2,1:T(8,128)(2,1)S(1)}, u32[]{:S(2)}, u32[]{:S(2)}) %all-to-all-start.1) | async-done | bytes 524320 | tf_op jit(solution)/shard_map/all_to_all | solution.py:103
  34.0 3.5 %all-to-all-start.3 = ((bf16[256,16,64]{0,2,1:T(8,128)(2,1)}), bf16[256,16,64]{0,2,1:T(8,128)(2,1)S(1)}, u32[]{:S(2)}, u32[]{:S(2)}) async-start(bf16[256,16,64]{0,2,1:T(8,128)(2,1)} %bitcast.202), calls=%async_computation.3 | async-start | bytes 1048576 | tf_op jit(solution)/shard_map/all_to_all | solution.py:104
  37.5 2.6 convolution_convert_fusion.1
  40.0 2.0 copy.144
  42.1 1.9 all-to-all-done.3
  44.0 4.1 %all-to-all-start.2 = ((bf16[256,16,64]{0,2,1:T(8,128)(2,1)}), bf16[256,16,64]{0,2,1:T(8,128)(2,1)}, u32[]{:S(2)}, u32[]{:S(2)}) async-start(bf16[256,16,64]{0,2,1:T(8,128)(2,1)} %bitcast.201), calls=%async_computation.2 | async-start | bytes 1048576 | tf_op jit(solution)/shard_map/all_to_all | solution.py:105
  49.5 2.2 copy.221
  51.8 2.0 reshape.159
  56.6 1.5 copy.220
  60.2 89.4 %while.17 = (s32[]{:T(128)}, f32[8,128,4,64]{1,3,2,0:T(8,128)}, f32[8,128,4,64]{1,3,2,0:T(8,128)S(1)}, bf16[2,4,128,4,64]{2,4,3,1,0:T(8,128)(2,1)}, bf16[2,4,128...) while((s32[]{:T(128)}, f32[8,128,4,64]{1,3,2,0:T(8,128)}, ...), condition=%wide.region_6.7_spmd.clone, body=%wide.region_0.6_spmd.clone.sunk | while | flops 832957568 | bytes 82146608 | solution.py:70
  60.5 1.9 constant_dynamic-slice_fusion.6
  62.4 4.8 %gather_fusion.1 = bf16[16,128,4,64]{3,2,1,0:T(4,128)(2,1)} fusion(bf16[8,128,4,64]{3,2,1,0:T(4,128)(2,1)} %get-tuple-element.318, s32[1024]{0:T(1024)S(1)} %pad_clamp_fusion.2), kind=kCustom, calls=%fused_computation.clone.clone.1 | custom fusion | bytes 2097216 | tf_op jit(solution)/shard_map/while/body/eval_jaxpr/gather | solution.py:41
  67.2 4.1 %copy.237 = bf16[4,4,128,4,64]{2,4,1,3,0:T(8,128)(2,1)} copy(bf16[4,4,128,4,64]{4,3,2,1,0:T(4,128)(2,1)} %bitcast.182) | data formatting | bytes 2097152 | tf_op jit(solution)/shard_map/while/body/eval_jaxpr/gather | solution.py:41
  71.2 4.8 %gather_fusion = bf16[16,128,4,64]{3,2,1,0:T(4,128)(2,1)} fusion(bf16[8,128,4,64]{3,2,1,0:T(4,128)(2,1)} %get-tuple-element.320, s32[1024]{0:T(1024)S(1)} %pad_clamp_fusion.2), kind=kCustom, calls=%fused_computation.1.clone.clone.1 | custom fusion | bytes 2097216 | tf_op jit(solution)/shard_map/while/body/eval_jaxpr/gather | solution.py:42
  76.0 4.0 %copy.236 = bf16[4,4,128,4,64]{2,4,1,3,0:T(8,128)(2,1)} copy(bf16[4,4,128,4,64]{4,3,2,1,0:T(4,128)(2,1)} %bitcast.181) | data formatting | bytes 2097152 | tf_op jit(solution)/shard_map/while/body/eval_jaxpr/gather | solution.py:42
  80.0 2.5 fusion.60
  85.6 2.0 multiply_convert_fusion.2
  87.6 2.6 convolution_bitcast_fusion.4
  91.6 1.4 copy.238
  93.1 5.1 %scatter_fusion = f32[8,128,4,64]{1,3,2,0:T(8,128)} fusion(f32[8,128,4,64]{1,3,2,0:T(8,128)} %get-tuple-element.299, s32[16]{0:T(128)S(1)} %fusion.58, f32[16,128,4,64]{1,3,2,0:T(8,128)} %bitcast.180), kind=kCustom, calls=%fused_computation.2.clone.clone.1 | custom fusion | flops 524288 | bytes 6291520 | tf_op jit(solution)/shard_map/while/body/eval_jaxpr/scatter-add | solution.py:61
  98.1 3.2 %copy.239 = f32[4,4,128,4,64]{2,4,3,1,0:T(8,128)} copy(f32[4,4,128,4,64]{2,4,1,3,0:T(8,128)} %convolution_bitcast_fusion.4) | data formatting | bytes 4194304 | tf_op jit(solution)/shard_map/while/body/eval_jaxpr/gnqjk,gqnd->gjknd/transpose | solution.py:15
  101.3 3.5 %scatter_fusion.1 = f32[8,128,4,64]{1,3,2,0:T(8,128)S(1)} fusion(f32[8,128,4,64]{1,3,2,0:T(8,128)S(1)} %get-tuple-element.300, s32[16]{0:T(128)S(1)} %fusion.58, f32[16,128,4,64]{1,3,2,0:T(8,128)} %bitcast.179), kind=kCustom, calls=%fused_computation.3.clone.clone.1 | custom fusion | flops 524288 | bytes 6291520 | tf_op jit(solution)/shard_map/while/body/eval_jaxpr/scatter-add | solution.py:64
  105.1 1.9 constant_dynamic-slice_fusion.6
  107.0 4.8 %gather_fusion.1 = bf16[16,128,4,64]{3,2,1,0:T(4,128)(2,1)} fusion(bf16[8,128,4,64]{3,2,1,0:T(4,128)(2,1)} %get-tuple-element.318, s32[1024]{0:T(1024)S(1)} %pad_clamp_fusion.2), kind=kCustom, calls=%fused_computation.clone.clone.1 | custom fusion | bytes 2097216 | tf_op jit(solution)/shard_map/while/body/eval_jaxpr/gather | solution.py:41
  111.8 4.1 %copy.237 = bf16[4,4,128,4,64]{2,4,1,3,0:T(8,128)(2,1)} copy(bf16[4,4,128,4,64]{4,3,2,1,0:T(4,128)(2,1)} %bitcast.182) | data formatting | bytes 2097152 | tf_op jit(solution)/shard_map/while/body/eval_jaxpr/gather | solution.py:41
  115.8 4.8 %gather_fusion = bf16[16,128,4,64]{3,2,1,0:T(4,128)(2,1)} fusion(bf16[8,128,4,64]{3,2,1,0:T(4,128)(2,1)} %get-tuple-element.320, s32[1024]{0:T(1024)S(1)} %pad_clamp_fusion.2), kind=kCustom, calls=%fused_computation.1.clone.clone.1 | custom fusion | bytes 2097216 | tf_op jit(solution)/shard_map/while/body/eval_jaxpr/gather | solution.py:42
  120.6 4.0 %copy.236 = bf16[4,4,128,4,64]{2,4,1,3,0:T(8,128)(2,1)} copy(bf16[4,4,128,4,64]{4,3,2,1,0:T(4,128)(2,1)} %bitcast.181) | data formatting | bytes 2097152 | tf_op jit(solution)/shard_map/while/body/eval_jaxpr/gather | solution.py:42
  124.6 2.5 fusion.60
  130.2 2.0 multiply_convert_fusion.2
  132.2 2.6 convolution_bitcast_fusion.4
  137.7 5.1 %scatter_fusion = f32[8,128,4,64]{1,3,2,0:T(8,128)} fusion(f32[8,128,4,64]{1,3,2,0:T(8,128)} %get-tuple-element.299, s32[16]{0:T(128)S(1)} %fusion.58, f32[16,128,4,64]{1,3,2,0:T(8,128)} %bitcast.180), kind=kCustom, calls=%fused_computation.2.clone.clone.1 | custom fusion | flops 524288 | bytes 6291520 | tf_op jit(solution)/shard_map/while/body/eval_jaxpr/scatter-add | solution.py:61
  142.7 3.2 %copy.239 = f32[4,4,128,4,64]{2,4,3,1,0:T(8,128)} copy(f32[4,4,128,4,64]{2,4,1,3,0:T(8,128)} %convolution_bitcast_fusion.4) | data formatting | bytes 4194304 | tf_op jit(solution)/shard_map/while/body/eval_jaxpr/gnqjk,gqnd->gjknd/transpose | solution.py:15
  145.9 3.5 %scatter_fusion.1 = f32[8,128,4,64]{1,3,2,0:T(8,128)S(1)} fusion(f32[8,128,4,64]{1,3,2,0:T(8,128)S(1)} %get-tuple-element.300, s32[16]{0:T(128)S(1)} %fusion.58, f32[16,128,4,64]{1,3,2,0:T(8,128)} %bitcast.179), kind=kCustom, calls=%fused_computation.3.clone.clone.1 | custom fusion | flops 524288 | bytes 6291520 | tf_op jit(solution)/shard_map/while/body/eval_jaxpr/scatter-add | solution.py:64
  149.6 2.3 copy.184
  151.9 2.6 reshape.235
  154.5 11.3 %all_to_all.120 = bf16[4,2,32768]{2,1,0:T(2,128)(2,1)} all-to-all(bf16[4,2,32768]{2,1,0:T(2,128)(2,1)} %reshape.235), channel_id=1, replica_groups=mesh['dp'=8,'seq'=4] {'seq'}, dimensions={0} | all-to-all | bytes 1048576 | tf_op jit(solution)/shard_map/all_to_all | solution.py:111
  165.8 2.5 reshape.236
  168.3 2.2 copy.156
  170.5 3.9 %fusion.22 = f32[1024,1024]{1,0:T(8,128)} fusion(bf16[256,1024]{0,1:T(8,128)(2,1)} %bitcast.185, bf16[1,256,1024]{2,1,0:T(8,128)(2,1)} %param.12), kind=kOutput, calls=%fused_computation.43 | convolution fusion | flops 536870912 | bytes 5242880 | tf_op jit(solution)/shard_map/dot_general | solution.py:19
  174.4 52.5 %reduce-scatter.3.cloned.1.call-done = f32[256,1024]{1,0:T(8,128)} async-done(((f32[1024,1024]{1,0:T(8,128)}), f32[256,1024]{1,0:T(8,128)}) %reduce-scatter.3.cloned.1.call-update) | async-done | bytes 1048592 | tf_op jit(solution)/shard_map/reduce_scatter | solution.py:119
  226.9 2.3 copy.187
  229.2 2.6 reshape.237
  231.8 4.1 %all-to-all-start.5 = ((bf16[4,2,32768]{2,1,0:T(2,128)(2,1)}), bf16[4,2,32768]{2,1,0:T(2,128)(2,1)}, u32[]{:S(2)}, u32[]{:S(2)}) async-start(bf16[4,2,32768]{2,1,0:T(2,128)(2,1)} %reshape.237), calls=%async_computation.5 | async-start | bytes 1048576 | tf_op jit(solution)/shard_map/all_to_all | solution.py:112
  235.9 2.1 convert_element_type.38
  238.0 2.3 copy.190
  240.3 2.6 reshape.239
  244.3 4.1 %all-to-all-start.6 = ((bf16[4,2,32768]{2,1,0:T(2,128)(2,1)}), bf16[4,2,32768]{2,1,0:T(2,128)(2,1)}, u32[]{:S(2)}, u32[]{:S(2)}) async-start(bf16[4,2,32768]{2,1,0:T(2,128)(2,1)} %reshape.239), calls=%async_computation.6 | async-start | bytes 1048576 | tf_op jit(solution)/shard_map/all_to_all | solution.py:113
  249.3 1.6 copy.193
  250.9 1.6 reshape.241
  252.5 3.5 %all-to-all-done.6 = bf16[4,2,32768]{2,1,0:T(2,128)(2,1)} async-done(((bf16[4,2,32768]{2,1,0:T(2,128)(2,1)}), bf16[4,2,32768]{2,1,0:T(2,128)(2,1)}, u32[]{:S(2)}, u32[]{:S(2)}) %all-to-all-start.6) | async-done | bytes 524320 | tf_op jit(solution)/shard_map/all_to_all | solution.py:113
  256.0 4.1 %all-to-all-start.7 = ((bf16[4,2,32768]{2,1,0:T(2,128)(2,1)}), bf16[4,2,32768]{2,1,0:T(2,128)(2,1)}, u32[]{:S(2)}, u32[]{:S(2)}) async-start(bf16[4,2,32768]{2,1,0:T(2,128)(2,1)} %reshape.241), calls=%async_computation.7 | async-start | bytes 1048576 | tf_op jit(solution)/shard_map/all_to_all | solution.py:114
  260.1 1.7 reshape.238
  263.1 2.0 copy.169
  265.1 2.6 reshape.240
  267.7 1.5 copy.164
  270.2 2.5 reshape.242
  272.8 1.5 copy.168
  275.2 1.5 fusion.21
  276.8 1.6 broadcast_multiply_fusion
  (81 shorter events, 24.6 us)
Async XLA Ops:
  7.2 30.3 %copy-start = (bf16[1024,1024]{1,0:T(8,128)(2,1)S(1)}, bf16[1024,1024]{1,0:T(8,128)(2,1)}, u32[]{:S(2)}) copy-start(bf16[1024,1024]{1,0:T(8,128)(2,1)} %param.13) | copy-start | bytes 6291460
  7.2 19.7 %copy-start.8 = (bf16[1,256,1024]{2,1,0:T(8,128)(2,1)S(1)}, bf16[1,256,1024]{2,1,0:T(8,128)(2,1)}, u32[]{:S(2)}) copy-start(bf16[1,256,1024]{2,1,0:T(8,128)(2,1)} %param.11) | copy-start | bytes 1572868
  9.4 13.2 %all-to-all-start = ((bf16[256,16,64]{0,2,1:T(8,128)(2,1)}), bf16[256,16,64]{0,2,1:T(8,128)(2,1)S(1)}, u32[]{:S(2)}, u32[]{:S(2)}) async-start(bf16[256,16,64]{0,2,1:T(8,128)(2,1)} %bitcast.1), calls=%async_computation | async-start | bytes 1048576 | tf_op jit(solution)/shard_map/all_to_all | solution.py:102
  22.6 0.8 copy-start.5
  22.6 26.1 %copy-start.10 = (s32[1,8]{1,0:T(1,128)S(1)}, s32[1,8]{1,0:T(1,128)}, u32[]{:S(2)}) copy-start(s32[1,8]{1,0:T(1,128)} %param.15) | copy-start | bytes 100
  22.6 26.9 %copy-start.9 = (s32[1,8,4]{1,2,0:T(4,128)S(1)}, s32[1,8,4]{1,2,0:T(4,128)}, u32[]{:S(2)}) copy-start(s32[1,8,4]{1,2,0:T(4,128)} %param.14) | copy-start | bytes 388
  23.4 10.6 %all-to-all-start.1 = ((bf16[256,16,64]{0,2,1:T(8,128)(2,1)}), bf16[256,16,64]{0,2,1:T(8,128)(2,1)S(1)}, u32[]{:S(2)}, u32[]{:S(2)}) async-start(bf16[256,16,64]{0,2,1:T(8,128)(2,1)} %bitcast.4), calls=%async_computation.1 | async-start | bytes 1048576 | tf_op jit(solution)/shard_map/all_to_all | solution.py:103
  34.0 10.0 %all-to-all-start.3 = ((bf16[256,16,64]{0,2,1:T(8,128)(2,1)}), bf16[256,16,64]{0,2,1:T(8,128)(2,1)S(1)}, u32[]{:S(2)}, u32[]{:S(2)}) async-start(bf16[256,16,64]{0,2,1:T(8,128)(2,1)} %bitcast.202), calls=%async_computation.3 | async-start | bytes 1048576 | tf_op jit(solution)/shard_map/all_to_all | solution.py:104
  44.0 12.6 %all-to-all-start.2 = ((bf16[256,16,64]{0,2,1:T(8,128)(2,1)}), bf16[256,16,64]{0,2,1:T(8,128)(2,1)}, u32[]{:S(2)}, u32[]{:S(2)}) async-start(bf16[256,16,64]{0,2,1:T(8,128)(2,1)} %bitcast.201), calls=%async_computation.2 | async-start | bytes 1048576 | tf_op jit(solution)/shard_map/all_to_all | solution.py:105
  48.1 178.8 %reduce-scatter.3.cloned.1.call-start = ((), (), s32[]{:S(2)}) async-start(), calls=%async_computation.10 | async-start | bytes 5242880 | tf_op jit(solution)/shard_map/reduce_scatter | solution.py:119
  80.0 3.4 %copy-start.2 = (bf16[4,4,128,4,64]{2,4,1,3,0:T(8,128)(2,1)S(1)}, bf16[4,4,128,4,64]{2,4,1,3,0:T(8,128)(2,1)}, u32[]{:S(2)}) copy-start(bf16[4,4,128,4,64]{2,4,1,3,0:T(8,128)(2,1)} %copy.236) | copy-start | bytes 3145732 | tf_op jit(solution)/shard_map/while
  80.0 3.4 %copy-start.4 = (bf16[1,4,128,4,64]{2,1,0,4,3:T(4,128)(2,1)S(1)}, bf16[1,4,128,4,64]{2,1,0,4,3:T(4,128)(2,1)}, u32[]{:S(2)}) copy-start(bf16[1,4,128,4,64]{2,1,0,4,3:T(4,128)(2,1)} %get-tuple-element.280) | copy-start | bytes 786436 | tf_op jit(solution)/shard_map/while
  87.6 2.6 copy-start.1
  87.6 2.6 copy-start.6
  90.7 2.3 copy-start.7
  124.6 3.4 %copy-start.2 = (bf16[4,4,128,4,64]{2,4,1,3,0:T(8,128)(2,1)S(1)}, bf16[4,4,128,4,64]{2,4,1,3,0:T(8,128)(2,1)}, u32[]{:S(2)}) copy-start(bf16[4,4,128,4,64]{2,4,1,3,0:T(8,128)(2,1)} %copy.236) | copy-start | bytes 3145732 | tf_op jit(solution)/shard_map/while
  124.6 3.4 %copy-start.4 = (bf16[1,4,128,4,64]{2,1,0,4,3:T(4,128)(2,1)S(1)}, bf16[1,4,128,4,64]{2,1,0,4,3:T(4,128)(2,1)}, u32[]{:S(2)}) copy-start(bf16[1,4,128,4,64]{2,1,0,4,3:T(4,128)(2,1)} %get-tuple-element.280) | copy-start | bytes 786436 | tf_op jit(solution)/shard_map/while
  132.2 2.6 copy-start.1
  132.2 2.6 copy-start.6
  135.3 2.3 copy-start.7
  174.4 102.4 %reduce-scatter.5.cloned.1.call-start = ((), (), s32[]{:S(2)}) async-start(), calls=%async_computation.11 | async-start | bytes 1179648 | tf_op jit(solution)/shard_map/reduce_scatter | solution.py:122
  231.8 12.5 %all-to-all-start.5 = ((bf16[4,2,32768]{2,1,0:T(2,128)(2,1)}), bf16[4,2,32768]{2,1,0:T(2,128)(2,1)}, u32[]{:S(2)}, u32[]{:S(2)}) async-start(bf16[4,2,32768]{2,1,0:T(2,128)(2,1)} %reshape.237), calls=%async_computation.5 | async-start | bytes 1048576 | tf_op jit(solution)/shard_map/all_to_all | solution.py:112
  244.3 11.7 %all-to-all-start.6 = ((bf16[4,2,32768]{2,1,0:T(2,128)(2,1)}), bf16[4,2,32768]{2,1,0:T(2,128)(2,1)}, u32[]{:S(2)}, u32[]{:S(2)}) async-start(bf16[4,2,32768]{2,1,0:T(2,128)(2,1)} %reshape.239), calls=%async_computation.6 | async-start | bytes 1048576 | tf_op jit(solution)/shard_map/all_to_all | solution.py:113
  256.0 14.3 %all-to-all-start.7 = ((bf16[4,2,32768]{2,1,0:T(2,128)(2,1)}), bf16[4,2,32768]{2,1,0:T(2,128)(2,1)}, u32[]{:S(2)}, u32[]{:S(2)}) async-start(bf16[4,2,32768]{2,1,0:T(2,128)(2,1)} %reshape.241), calls=%async_computation.7 | async-start | bytes 1048576 | tf_op jit(solution)/shard_map/all_to_all | solution.py:114
  265.1 10.1 %copy-start.3 = (bf16[256,4,4,64]{0,3,2,1:T(8,128)(2,1)S(1)}, bf16[256,4,4,64]{0,3,2,1:T(8,128)(2,1)}, u32[]{:S(2)}) copy-start(bf16[256,4,4,64]{0,3,2,1:T(8,128)(2,1)} %copy.156) | copy-start | bytes 1572868
Sparse Core Ops, SparseCore 0:
  174.5 52.3 reduce-scatter.2
  229.3 32.0 reduce-scatter.4
where the time goes:
time: 287 us; the launch traced here: 285 us
  local copies, waits for them, and re-layouts  107 us (37%)
  waiting for transfers between devices  71.4 us (25%)
  starting transfers between devices  28.7 us (10%)
  matrix products  27.7 us (10%)
  other arithmetic  24.3 us (8%)
  between operations  14.2 us (5%)
  blocking collectives  11.3 us (4%)
    reduce_scatter x1, waiting for transfers between devices, local(): lax.psum_scatter(inner_rows(att_nodes, up_rows), 'seq', scatter_dimension...  52.5 us
    unnamed x30, local copies, waits for them, and re-layouts  32.1 us
    dot_general x12, matrix products, product(): return jnp.einsum(form, left, right, preferred_element_type=jnp.float32)  19.7 us
    gather x4, local copies, waits for them, and re-layouts, one_step(): keys_near = key_table[list_part]  17.7 us
    gather x4, local copies, waits for them, and re-layouts, one_step(): values_near = value_table[list_part]  17.6 us
    all_to_all x1, blocking collectives, local(): lax.all_to_all(attended, 'seq', split_axis=0, concat_axis=1, tiled=True)  11.3 us
    scatter-add x2, other arithmetic, one_step(): key_acc.at[flat_list]  10.1 us
    scatter-add x2, other arithmetic, one_step(): value_acc.at[flat_list]  7 us
  transfers between devices with their start and end apart: 9, of which 6 were waited for; matrix products, arithmetic and copies ran while one was open for 17% of the time, Pallas kernels for 0%

commit v1 on v0

--- a/solution.py
+++ b/solution.py
@@ -1,8 +1,11 @@
+import functools
 import math
 
 import jax
 import jax.numpy as jnp
 from jax import lax
+from jax.experimental import pallas as pl
+from jax.experimental.pallas import tpu as pltpu
 from jax.sharding import PartitionSpec as P
 
 HEADS = 16
@@ -85,7 +88,7 @@
     ).astype(jnp.bfloat16)
 
 
-def local(queries, keys, values, upstream, w_out, key_blocks, block_counts):
+def local_plain(queries, keys, values, upstream, w_out, key_blocks, block_counts):
     local_rows = queries.shape[1]
     width = queries.shape[2]
     head_width = width // HEADS
@@ -128,6 +131,252 @@
         node_gv.reshape(full_shape),
         grad_wo * factor,
     )
+
+
+MESH = pl.DeviceIdType.MESH
+LANES = 128
+MASKED = -1e30
+
+
+def dot_nt(left, right):
+    return lax.dot_general(
+        left, right, (((1,), (1,)), ((), ())), preferred_element_type=jnp.float32
+    )
+
+
+def fused(
+    peers, head_width, list_ref, count_ref, q_ref, k_ref, v_ref, u_ref, w_ref,
+    mixed_ref, gq_ref, gk_ref, gv_ref, gw_ref,
+    head_q, head_g, keys2, values2, g_local, out_stage, key_sum, value_sum, att_nodes,
+    send_in, recv_in, send_out, recv_out, own_sem,
+):
+    me = lax.axis_index("seq")
+    rows = q_ref.shape[0]
+    chunks = head_q.shape[0]
+    nodes = head_q.shape[1]
+    blocks, listed = list_ref.shape
+    block_rows = nodes // blocks
+    per_device = blocks // peers
+    span = chunks * LANES
+    score_scale = 1.0 / math.sqrt(head_width)
+    bf16, f32 = jnp.bfloat16, jnp.float32
+
+    barrier = pltpu.get_barrier_semaphore()
+    for p in range(1, peers):
+        pl.semaphore_signal(
+            barrier, inc=1, device_id={"seq": lax.rem(me + p, peers)}, device_id_type=MESH
+        )
+    pl.semaphore_wait(barrier, peers - 1)
+
+    own_rows = pl.ds(pl.multiple_of(me * rows, rows), rows)
+
+    def columns(device, c):
+        return pl.ds(pl.multiple_of(device * span + c * LANES, LANES), LANES)
+
+    sources = (q_ref, k_ref, v_ref, g_local)
+    targets = (head_q, keys2, values2, head_g)
+
+    def landing(a, c):
+        if a in (1, 2):
+            return targets[a].at[c, own_rows, pl.ds(0, LANES)]
+        return targets[a].at[c, own_rows]
+
+    def inward(a, c, p):
+        device = lax.rem(me + p, peers)
+        return pltpu.make_async_remote_copy(
+            src_ref=sources[a].at[:, columns(device, c)],
+            dst_ref=landing(a, c),
+            send_sem=send_in.at[c, a, p - 1],
+            recv_sem=recv_in.at[c, a, p - 1],
+            device_id={"seq": device},
+            device_id_type=MESH,
+        )
+
+    def own_copy(a, c):
+        return pltpu.make_async_copy(
+            sources[a].at[:, columns(me, c)], landing(a, c), own_sem.at[c, a]
+        )
+
+    def start_in(a, c):
+        for p in range(1, peers):
+            inward(a, c, p).start()
+        own_copy(a, c).start()
+
+    def finish_in(a, c):
+        for p in range(1, peers):
+            inward(a, c, p).wait()
+        own_copy(a, c).wait()
+
+    returns = (att_nodes, gq_ref, gk_ref, gv_ref)
+
+    def outward(a, c, p):
+        device = lax.rem(me + p, peers)
+        return pltpu.make_async_remote_copy(
+            src_ref=out_stage.at[c, a, pl.ds(pl.multiple_of(device * rows, rows), rows)],
+            dst_ref=returns[a].at[:, columns(me, c)],
+            send_sem=send_out.at[c, a, p - 1],
+            recv_sem=recv_out.at[c, a, p - 1],
+            device_id={"seq": device},
+            device_id_type=MESH,
+        )
+
+    def keep_own(a, c):
+        returns[a][:, columns(me, c)] = out_stage[c, a, own_rows, :]
+
+    def grad_att(c):
+        def one(device, carry):
+            cols = columns(device, c)
+            g_local[:, cols] = dot_nt(u_ref[...], w_ref[cols, :]).astype(bf16)
+            return carry
+
+        lax.fori_loop(0, peers, one, 0)
+
+    lane = lax.broadcasted_iota(jnp.int32, (block_rows, LANES), 1)
+    lane2 = lax.broadcasted_iota(jnp.int32, (2 * block_rows, LANES), 1)
+    first = lane < head_width
+
+    def stacked(x):
+        return jnp.concatenate([jnp.where(first, x, 0.0), jnp.where(first, 0.0, x)], axis=0)
+
+    def merged(x):
+        return jnp.where(first, x[:block_rows], x[block_rows:])
+
+    def attend(c):
+        key_sum[...] = jnp.zeros_like(key_sum)
+        value_sum[...] = jnp.zeros_like(value_sum)
+
+        def one_block(i, carry):
+            p = i // per_device + 1
+            b = lax.rem(me + p, peers) * per_device + lax.rem(i, per_device)
+            here = pl.ds(pl.multiple_of(b * block_rows, block_rows), block_rows)
+            q = head_q[c, here, :].astype(f32) * score_scale
+            g = head_g[c, here, :].astype(f32)
+            count = count_ref[b]
+            used = lane2 < 0
+            for j in range(listed):
+                used = used | (lane2 == jnp.where(j < count, list_ref[b, j], -1))
+            q_pair = stacked(q)
+            g_pair = stacked(g)
+            left = jnp.concatenate([q_pair, jnp.where(used, 0.0, MASKED)], axis=1).astype(bf16)
+            scores = dot_nt(left, keys2[c])
+            raised = jnp.exp(scores - jnp.max(scores, axis=1, keepdims=True))
+            weights = raised.astype(bf16)
+            summed = jnp.dot(weights, values2[c], preferred_element_type=f32)
+            inverse = 1.0 / summed[:, LANES:LANES + 1]
+            attended = merged(summed[:, :LANES] * inverse).astype(bf16)
+            delta = jnp.sum(
+                g_pair * jnp.concatenate([attended, attended], axis=0).astype(f32),
+                axis=1, keepdims=True,
+            )
+            high = delta.astype(bf16).astype(f32)
+            middle = (delta - high).astype(bf16).astype(f32)
+            low = delta - high - middle
+            shift = jnp.where(
+                lane2 == 0, -high, jnp.where(lane2 == 1, -middle, jnp.where(lane2 == 2, -low, 0.0))
+            )
+            right = jnp.concatenate([g_pair, shift], axis=1).astype(bf16)
+            shifted = dot_nt(right, values2[c])
+            logits = (raised * shifted).astype(bf16)
+            grad_q = jnp.dot(logits, keys2[c, :, :LANES], preferred_element_type=f32)
+            grad_q = merged(grad_q * (inverse * score_scale))
+            key_sum[...] += inner_rows((q_pair * inverse).astype(bf16), logits)
+            value_sum[...] += inner_rows((g_pair * inverse).astype(bf16), weights)
+            out_stage[c, 0, here, :] = attended
+            out_stage[c, 1, here, :] = grad_q.astype(bf16)
+
+            @pl.when((lax.rem(i, per_device) == per_device - 1) & (p < peers))
+            def _():
+                outward(0, c, p).start()
+                outward(1, c, p).start()
+
+            return carry
+
+        lax.fori_loop(0, blocks, one_block, 0)
+        out_stage[c, 2] = key_sum[...].T.astype(bf16)
+        out_stage[c, 3] = value_sum[...].T.astype(bf16)
+        for p in range(1, peers):
+            outward(2, c, p).start()
+            outward(3, c, p).start()
+        for a in range(4):
+            keep_own(a, c)
+
+    for a in range(3):
+        start_in(a, 0)
+    grad_att(0)
+    start_in(3, 0)
+    for c in range(1, chunks):
+        grad_att(c)
+    block_of = lax.broadcasted_iota(jnp.int32, (nodes, LANES), 0) // block_rows
+    node_lane = lax.broadcasted_iota(jnp.int32, (nodes, LANES), 1)
+    for c in range(chunks):
+        keys2[c, :, LANES:] = jnp.where(node_lane == block_of, 1.0, 0.0).astype(bf16)
+        values2[c, :, LANES:] = jnp.where(node_lane < 3, 1.0, 0.0).astype(bf16)
+    for c in range(chunks):
+        for a in range(4):
+            if a == 3 and c + 1 < chunks:
+                for later in range(4):
+                    start_in(later, c + 1)
+            finish_in(a, c)
+        attend(c)
+    for c in range(chunks):
+        for p in range(1, peers):
+            outward(0, c, p).wait()
+    mixed_ref[...] = jnp.dot(att_nodes[...], w_ref[...], preferred_element_type=f32).astype(bf16)
+    gw_ref[...] = inner_rows(att_nodes[...], u_ref[...])
+    for c in range(chunks):
+        for a in range(1, 4):
+            for p in range(1, peers):
+                outward(a, c, p).wait()
+
+
+def local_fused(queries, keys, values, upstream, w_out, key_blocks, block_counts):
+    rows, width = queries.shape[1:]
+    peers = lax.axis_size("seq")
+    chunks = width // peers // LANES
+    nodes = rows * peers
+    bf16, f32 = jnp.bfloat16, jnp.float32
+    vmem = pl.BlockSpec(memory_space=pltpu.VMEM)
+    smem = pl.BlockSpec(memory_space=pltpu.SMEM)
+    part = jax.ShapeDtypeStruct((rows, width), bf16)
+    mixed, grad_q, grad_k, grad_v, partial = pl.pallas_call(
+        functools.partial(fused, peers, width // HEADS),
+        out_shape=(part, part, part, part, jax.ShapeDtypeStruct((width, width), f32)),
+        in_specs=[smem, smem] + [vmem] * 5,
+        out_specs=[vmem] * 5,
+        scratch_shapes=[
+            pltpu.VMEM((chunks, nodes, LANES), bf16),
+            pltpu.VMEM((chunks, nodes, LANES), bf16),
+            pltpu.VMEM((chunks, nodes, 2 * LANES), bf16),
+            pltpu.VMEM((chunks, nodes, 2 * LANES), bf16),
+            pltpu.VMEM((rows, width), bf16),
+            pltpu.VMEM((chunks, 4, nodes, LANES), bf16),
+            pltpu.VMEM((LANES, nodes), f32),
+            pltpu.VMEM((LANES, nodes), f32),
+            pltpu.VMEM((rows, width), bf16),
+            pltpu.SemaphoreType.DMA((chunks, 4, peers - 1)),
+            pltpu.SemaphoreType.DMA((chunks, 4, peers - 1)),
+            pltpu.SemaphoreType.DMA((chunks, 4, peers - 1)),
+            pltpu.SemaphoreType.DMA((chunks, 4, peers - 1)),
+            pltpu.SemaphoreType.DMA((chunks, 4)),
+        ],
+        compiler_params=pltpu.CompilerParams(
+            collective_id=0, has_side_effects=True, vmem_limit_bytes=56 * 1024 * 1024
+        ),
+        name="graph_attention",
+    )(key_blocks[0], block_counts[0], queries[0], keys[0], values[0], upstream[0], w_out)
+    factor = 1.0 / math.sqrt(lax.axis_size("dp") * nodes)
+    summed = lax.psum_scatter(partial, "seq", scatter_dimension=0, tiled=True)
+    grad_wo = lax.psum_scatter(summed, "dp", scatter_dimension=1, tiled=True)
+    return mixed[None], grad_q[None], grad_k[None], grad_v[None], grad_wo * factor
+
+
+def local(queries, keys, values, upstream, w_out, key_blocks, block_counts):
+    width = queries.shape[2]
+    peers = lax.axis_size("seq")
+    pair = 2 * (width // HEADS) == LANES and width % (peers * LANES) == 0
+    whole_blocks = key_blocks.shape[1] % peers == 0 and key_blocks.shape[1] <= LANES
+    chosen = local_fused if pair and whole_blocks else local_plain
+    return chosen(queries, keys, values, upstream, w_out, key_blocks, block_counts)
 
 
 def solution(mesh):

time: 287 us -> 165 us (0.57)
  local copies, waits for them, and re-layouts: 107 us -> 4.54 us
  Pallas kernels: 0 us -> 55.8 us
  starting transfers between devices: 28.7 us -> 0.08 us
  matrix products: 27.7 us -> 0 us
  other arithmetic: 24.3 us -> 1.57 us
  waiting for transfers between devices: 71.4 us -> 88.5 us
  blocking collectives: 11.3 us -> 0 us
    pallas_call x0 -> x1, Pallas kernels: none -> 55.8 us  [local_fused(): pl.pallas_call(functools.partial(fused, peers, width // HEADS), out_shape...]
    reduce_scatter x2, waiting for transfers between devices: 52.5 us -> 88.4 us  [the longest x1 53.8 us: local_fused(): summed = lax.psum_scatter(partial, 'seq', scatter_dimension=0, tiled=True)]
    gather x8 -> x0, local copies, waits for them, and re-layouts: 35.3 us -> none  [the longest x4 17.7 us: one_step(): keys_near = key_table[list_part]]
    unnamed x30 -> x12, local copies, waits for them, and re-layouts: 32.1 us -> 3.19 us
    all_to_all x7 -> x0, starting transfers between devices: 28.6 us -> none  [the longest x1 5.16 us: local(): lax.all_to_all(query_heads, 'seq', split_axis=1, concat_axis=0, tiled=True)]
    dot_general x15 -> x0, matrix products: 27.7 us -> none  [the longest x12 19.7 us: product(): return jnp.einsum(form, left, right, preferred_element_type=jnp.float32)]
    all_to_all x7 -> x0, waiting for transfers between devices: 18.9 us -> none  [the longest x1 6.11 us: local(): lax.all_to_all(key_heads, 'seq', split_axis=1, concat_axis=0, tiled=True)]
    scatter-add x4 -> x0, other arithmetic: 17.1 us -> none  [the longest x2 10.1 us: one_step(): key_acc.at[flat_list]]
  transfers between devices with their start and end apart: 9 -> 2, of which waited for: 6 -> 2; matrix products, arithmetic and copies ran while one was open for 17% -> 0% of each run, Pallas kernels for 0% -> 0%
where the time goes in v1:
time: 165 us; the launch traced here: 164 us
  waiting for transfers between devices  88.5 us (54%)
  Pallas kernels  55.8 us (34%)
  between operations  14.1 us (9%)
  local copies, waits for them, and re-layouts  4.54 us (3%)
    pallas_call x1, Pallas kernels, local_fused(): pl.pallas_call(functools.partial(fused, peers, width // HEADS), out_shape...  55.8 us
    reduce_scatter x1, waiting for transfers between devices, local_fused(): summed = lax.psum_scatter(partial, 'seq', scatter_dimension=0, tiled=True)  53.8 us
    reduce_scatter x1, waiting for transfers between devices, local_fused(): grad_wo = lax.psum_scatter(summed, 'dp', scatter_dimension=1, tiled=True)  34.6 us
  transfers between devices with their start and end apart: 2, of which 2 were waited for; matrix products, arithmetic and copies ran while one was open for 0% of the time, Pallas kernels for 0%

profile of v1, /device:TPU:0, one launch (start us, length us, event | category | flops | bytes accessed | tf_op | source)
XLA Modules:
  0.0 164.5 jit_solution(2192842913353343208)
XLA Ops:
  7.2 0.0 reduce-scatter.3.cloned.1.call-start
  7.2 1.3 copy.12.list_ref
  8.6 55.8 %graph_attention.1 = (bf16[256,1024]{1,0:T(8,128)(2,1)}, bf16[256,1024]{1,0:T(8,128)(2,1)}, bf16[256,1024]{1,0:T(8,128)(2,1)}, bf16[256,1024]{1,0:T(8,128)(2,1)}, f32[1024,1024]{1,0:T(8,128)}) custom-call(s32[8,4]{1,0:T(8,128)} %copy.12.list_ref, s32[8]{0:T(128)} %bitcast.19, bf16[256,1024]{1,0:T(8,128)(2,1)} %bitcast.10, bf16[256,1024]{1,0:T(8,128)(2,1)} %bitcast.11, ...), custom_call_target="tpu_custom_call" | custom-call | tf_op jit(solution)/shard_map/graph_attention/pallas_call | solution.py:341
  64.3 0.0 copy-start.3
  64.3 0.0 copy-start.2
  64.3 0.0 copy-start.1
  64.4 0.0 copy-start
  64.4 0.0 reduce-scatter.3.cloned.1.call-update
  64.4 0.0 reduce-scatter.5.cloned.1.call-start
  64.4 53.8 %reduce-scatter.3.cloned.1.call-done = f32[256,1024]{1,0:T(8,128)} async-done(((f32[1024,1024]{1,0:T(8,128)}), f32[256,1024]{1,0:T(8,128)}) %reduce-scatter.3.cloned.1.call-update) | async-done | bytes 1048592 | tf_op jit(solution)/shard_map/reduce_scatter | solution.py:368
  118.2 0.0 reduce-scatter.5.cloned.1.call-update
  118.3 34.6 %reduce-scatter.5.cloned.1.call-done = f32[256,128]{1,0:T(8,128)} async-done(((f32[256,1024]{1,0:T(8,128)}), f32[256,128]{1,0:T(8,128)}) %reduce-scatter.5.cloned.1.call-update) | async-done | bytes 131088 | tf_op jit(solution)/shard_map/reduce_scatter | solution.py:369
  152.9 1.6 broadcast_multiply_fusion
  154.5 0.0 copy-done.3
  154.5 0.8 copy.17
  155.3 0.0 copy-done.2
  155.3 0.8 copy.18
  156.0 0.0 copy-done.1
  156.1 0.8 copy.19
  156.8 0.0 copy-done
  156.8 0.8 copy.20
Async XLA Ops:
  7.2 111.1 %reduce-scatter.3.cloned.1.call-start = ((), (), s32[]{:S(2)}) async-start(), calls=%async_computation.2 | async-start | bytes 5242880 | tf_op jit(solution)/shard_map/reduce_scatter | solution.py:368
  64.3 90.1 %copy-start.3 = (bf16[256,1024]{1,0:T(8,128)(2,1)S(1)}, bf16[256,1024]{1,0:T(8,128)(2,1)}, u32[]{:S(2)}) copy-start(bf16[256,1024]{1,0:T(8,128)(2,1)} %get-tuple-element.10) | copy-start | bytes 1572868
  64.3 90.9 %copy-start.2 = (bf16[256,1024]{1,0:T(8,128)(2,1)S(1)}, bf16[256,1024]{1,0:T(8,128)(2,1)}, u32[]{:S(2)}) copy-start(bf16[256,1024]{1,0:T(8,128)(2,1)} %get-tuple-element.11) | copy-start | bytes 1572868
  64.3 91.7 %copy-start.1 = (bf16[256,1024]{1,0:T(8,128)(2,1)S(1)}, bf16[256,1024]{1,0:T(8,128)(2,1)}, u32[]{:S(2)}) copy-start(bf16[256,1024]{1,0:T(8,128)(2,1)} %get-tuple-element.12) | copy-start | bytes 1572868
  64.4 92.5 %copy-start = (bf16[256,1024]{1,0:T(8,128)(2,1)S(1)}, bf16[256,1024]{1,0:T(8,128)(2,1)}, u32[]{:S(2)}) copy-start(bf16[256,1024]{1,0:T(8,128)(2,1)} %get-tuple-element.13) | copy-start | bytes 1572868
  64.4 88.5 %reduce-scatter.5.cloned.1.call-start = ((), (), s32[]{:S(2)}) async-start(), calls=%async_computation.3 | async-start | bytes 1179648 | tf_op jit(solution)/shard_map/reduce_scatter | solution.py:369
Sparse Core Ops, SparseCore 0:
  64.5 53.6 reduce-scatter.2
  120.6 32.2 reduce-scatter.4

commit v2 on v1

--- a/solution.py
+++ b/solution.py
@@ -145,12 +145,17 @@
 
 
 def fused(
-    peers, head_width, list_ref, count_ref, q_ref, k_ref, v_ref, u_ref, w_ref,
+    peers, levels, head_width, factor, list_ref, count_ref, q_ref, k_ref, v_ref, u_ref, w_ref,
     mixed_ref, gq_ref, gk_ref, gv_ref, gw_ref,
     head_q, head_g, keys2, values2, g_local, out_stage, key_sum, value_sum, att_nodes,
+    gw_other, gw_own, gw_core, gw_level, gw_levels, gw_seq, gw_seqs,
     send_in, recv_in, send_out, recv_out, own_sem,
+    send_core, recv_core, send_level, recv_level, send_seq, recv_seq,
 ):
     me = lax.axis_index("seq")
+    replica = lax.axis_index("dp")
+    core = lax.rem(replica, 2)
+    level = replica // 2
     rows = q_ref.shape[0]
     chunks = head_q.shape[0]
     nodes = head_q.shape[1]
@@ -166,7 +171,17 @@
         pl.semaphore_signal(
             barrier, inc=1, device_id={"seq": lax.rem(me + p, peers)}, device_id_type=MESH
         )
-    pl.semaphore_wait(barrier, peers - 1)
+    other_core = level * 2 + 1 - core
+
+    def level_at(p):
+        return lax.rem(level + p, levels)
+
+    pl.semaphore_signal(barrier, inc=1, device_id={"dp": other_core}, device_id_type=MESH)
+    for p in range(1, levels):
+        pl.semaphore_signal(
+            barrier, inc=1, device_id={"dp": level_at(p) * 2 + core}, device_id_type=MESH
+        )
+    pl.semaphore_wait(barrier, peers + levels - 1)
 
     own_rows = pl.ds(pl.multiple_of(me * rows, rows), rows)
 
@@ -241,7 +256,87 @@
     def merged(x):
         return jnp.where(first, x[:block_rows], x[block_rows:])
 
-    def attend(c):
+    def core_copy(c):
+        return pltpu.make_async_remote_copy(
+            src_ref=gw_other.at[c], dst_ref=gw_core.at[c],
+            send_sem=send_core.at[c], recv_sem=recv_core.at[c],
+            device_id={"dp": other_core}, device_id_type=MESH,
+        )
+
+    def level_copy(c, p):
+        return pltpu.make_async_remote_copy(
+            src_ref=gw_level.at[c, level_at(p)], dst_ref=gw_levels.at[c, p - 1],
+            send_sem=send_level.at[c, p - 1], recv_sem=recv_level.at[c, p - 1],
+            device_id={"dp": level_at(p) * 2 + core}, device_id_type=MESH,
+        )
+
+    def seq_copy(c, p):
+        device = lax.rem(me + p, peers)
+        return pltpu.make_async_remote_copy(
+            src_ref=gw_seq.at[c, pl.ds(pl.multiple_of(device * LANES, LANES), LANES)],
+            dst_ref=gw_seqs.at[c, p - 1],
+            send_sem=send_seq.at[c, p - 1], recv_sem=recv_seq.at[c, p - 1],
+            device_id={"seq": device}, device_id_type=MESH,
+        )
+
+    def gw_partial(c):
+        for p in range(1, peers):
+            outward(0, c, p).wait()
+
+        def up_columns(which):
+            return jnp.concatenate(
+                [
+                    u_ref[:, pl.ds(pl.multiple_of((at * 2 + which) * LANES, LANES), LANES)]
+                    for at in range(levels)
+                ],
+                axis=1,
+            )
+
+        def one(device, carry):
+            place = pl.ds(pl.multiple_of(device * LANES, LANES), LANES)
+            att = att_nodes[:, columns(device, c)]
+            theirs = inner_rows(att, up_columns(1 - core)).astype(bf16)
+            ours = inner_rows(att, up_columns(core))
+            for at in range(levels):
+                cut = slice(at * LANES, (at + 1) * LANES)
+                gw_other[c, at, place, :] = theirs[:, cut]
+                gw_own[c, at, place, :] = ours[:, cut]
+            return carry
+
+        lax.fori_loop(0, peers, one, 0)
+        core_copy(c).start()
+
+    def gw_across_levels(c):
+        core_copy(c).wait()
+
+        def one(at, carry):
+            total = gw_own[c, at] + gw_core[c, at].astype(f32)
+            gw_own[c, at] = total
+            gw_level[c, at] = total.astype(bf16)
+            return carry
+
+        lax.fori_loop(0, levels, one, 0)
+        for p in range(1, levels):
+            level_copy(c, p).start()
+
+    def gw_across_seq(c):
+        total = gw_own[c, level]
+        for p in range(1, levels):
+            level_copy(c, p).wait()
+            total = total + gw_levels[c, p - 1].astype(f32)
+        gw_own[c, level] = total
+        gw_seq[c] = total.astype(bf16)
+        for p in range(1, peers):
+            seq_copy(c, p).start()
+
+    def gw_finish(c):
+        total = gw_own[c, level, pl.ds(pl.multiple_of(me * LANES, LANES), LANES), :]
+        for p in range(1, peers):
+            seq_copy(c, p).wait()
+            total = total + gw_seqs[c, p - 1].astype(f32)
+        gw_ref[c * LANES:(c + 1) * LANES, :] = total * factor
+
+    def attend(c, between):
         key_sum[...] = jnp.zeros_like(key_sum)
         value_sum[...] = jnp.zeros_like(value_sum)
 
@@ -289,6 +384,8 @@
                 outward(0, c, p).start()
                 outward(1, c, p).start()
 
+            for at, step in between:
+                pl.when(i == at)(step)
             return carry
 
         lax.fori_loop(0, blocks, one_block, 0)
@@ -317,16 +414,25 @@
                 for later in range(4):
                     start_in(later, c + 1)
             finish_in(a, c)
-        attend(c)
-    for c in range(chunks):
-        for p in range(1, peers):
-            outward(0, c, p).wait()
+        between = []
+        if c > 0:
+            between = [
+                (blocks // 4, functools.partial(gw_partial, c - 1)),
+                (blocks // 2, functools.partial(gw_across_levels, c - 1)),
+                (blocks - 2, functools.partial(gw_across_seq, c - 1)),
+            ]
+        attend(c, between)
+        if c > 0:
+            gw_finish(c - 1)
+    gw_partial(chunks - 1)
     mixed_ref[...] = jnp.dot(att_nodes[...], w_ref[...], preferred_element_type=f32).astype(bf16)
-    gw_ref[...] = inner_rows(att_nodes[...], u_ref[...])
+    gw_across_levels(chunks - 1)
     for c in range(chunks):
         for a in range(1, 4):
             for p in range(1, peers):
                 outward(a, c, p).wait()
+    gw_across_seq(chunks - 1)
+    gw_finish(chunks - 1)
 
 
 def local_fused(queries, keys, values, upstream, w_out, key_blocks, block_counts):
@@ -335,12 +441,15 @@
     chunks = width // peers // LANES
     nodes = rows * peers
     bf16, f32 = jnp.bfloat16, jnp.float32
+    replicas = lax.axis_size("dp")
+    levels = replicas // 2
+    factor = 1.0 / math.sqrt(replicas * nodes)
     vmem = pl.BlockSpec(memory_space=pltpu.VMEM)
     smem = pl.BlockSpec(memory_space=pltpu.SMEM)
     part = jax.ShapeDtypeStruct((rows, width), bf16)
-    mixed, grad_q, grad_k, grad_v, partial = pl.pallas_call(
-        functools.partial(fused, peers, width // HEADS),
-        out_shape=(part, part, part, part, jax.ShapeDtypeStruct((width, width), f32)),
+    mixed, grad_q, grad_k, grad_v, grad_wo = pl.pallas_call(
+        functools.partial(fused, peers, levels, width // HEADS, factor),
+        out_shape=(part, part, part, part, jax.ShapeDtypeStruct((chunks * LANES, width // replicas), f32)),
         in_specs=[smem, smem] + [vmem] * 5,
         out_specs=[vmem] * 5,
         scratch_shapes=[
@@ -353,21 +462,31 @@
             pltpu.VMEM((LANES, nodes), f32),
             pltpu.VMEM((LANES, nodes), f32),
             pltpu.VMEM((rows, width), bf16),
+            pltpu.VMEM((chunks, levels, peers * LANES, LANES), bf16),
+            pltpu.VMEM((chunks, levels, peers * LANES, LANES), f32),
+            pltpu.VMEM((chunks, levels, peers * LANES, LANES), bf16),
+            pltpu.VMEM((chunks, levels, peers * LANES, LANES), bf16),
+            pltpu.VMEM((chunks, levels - 1, peers * LANES, LANES), bf16),
+            pltpu.VMEM((chunks, peers * LANES, LANES), bf16),
+            pltpu.VMEM((chunks, peers - 1, LANES, LANES), bf16),
             pltpu.SemaphoreType.DMA((chunks, 4, peers - 1)),
             pltpu.SemaphoreType.DMA((chunks, 4, peers - 1)),
             pltpu.SemaphoreType.DMA((chunks, 4, peers - 1)),
             pltpu.SemaphoreType.DMA((chunks, 4, peers - 1)),
             pltpu.SemaphoreType.DMA((chunks, 4)),
+            pltpu.SemaphoreType.DMA((chunks,)),
+            pltpu.SemaphoreType.DMA((chunks,)),
+            pltpu.SemaphoreType.DMA((chunks, levels - 1)),
+            pltpu.SemaphoreType.DMA((chunks, levels - 1)),
+            pltpu.SemaphoreType.DMA((chunks, peers - 1)),
+            pltpu.SemaphoreType.DMA((chunks, peers - 1)),
         ],
         compiler_params=pltpu.CompilerParams(
             collective_id=0, has_side_effects=True, vmem_limit_bytes=56 * 1024 * 1024
         ),
         name="graph_attention",
     )(key_blocks[0], block_counts[0], queries[0], keys[0], values[0], upstream[0], w_out)
-    factor = 1.0 / math.sqrt(lax.axis_size("dp") * nodes)
-    summed = lax.psum_scatter(partial, "seq", scatter_dimension=0, tiled=True)
-    grad_wo = lax.psum_scatter(summed, "dp", scatter_dimension=1, tiled=True)
-    return mixed[None], grad_q[None], grad_k[None], grad_v[None], grad_wo * factor
+    return mixed[None], grad_q[None], grad_k[None], grad_v[None], grad_wo
 
 
 def local(queries, keys, values, upstream, w_out, key_blocks, block_counts):
@@ -375,7 +494,8 @@
     peers = lax.axis_size("seq")
     pair = 2 * (width // HEADS) == LANES and width % (peers * LANES) == 0
     whole_blocks = key_blocks.shape[1] % peers == 0 and key_blocks.shape[1] <= LANES
-    chosen = local_fused if pair and whole_blocks else local_plain
+    columns_fit = lax.axis_size("dp") * LANES == width
+    chosen = local_fused if pair and whole_blocks and columns_fit else local_plain
     return chosen(queries, keys, values, upstream, w_out, key_blocks, block_counts)
 
 

time: 165 us -> 88.1 us (0.53)
  waiting for transfers between devices: 88.5 us -> 0 us
  Pallas kernels: 55.8 us -> 79.5 us
  between operations: 14.1 us -> 0.67 us
  local copies, waits for them, and re-layouts: 4.54 us -> 7.43 us
    reduce_scatter x2 -> x0, waiting for transfers between devices: 88.4 us -> none  [the longest x1 53.8 us: local_fused(): summed = lax.psum_scatter(partial, 'seq', scatter_dimension=0, tiled=True)]
    pallas_call x1, Pallas kernels: 55.8 us -> 79.5 us  [local_fused(): pl.pallas_call(functools.partial(fused, peers, levels, width // HEADS, fa...]
    unnamed x12 -> x11, local copies, waits for them, and re-layouts: 3.19 us -> 6.08 us
  transfers between devices with their start and end apart: 2 -> 0, of which waited for: 2 -> 0; matrix products, arithmetic and copies ran while one was open for 0% -> 0% of each run, Pallas kernels for 0% -> 0%
where the time goes in v2:
time: 88.1 us; the launch traced here: 87.6 us
  Pallas kernels  79.5 us (90%)
  local copies, waits for them, and re-layouts  7.43 us (8%)
    pallas_call x1, Pallas kernels, local_fused(): pl.pallas_call(functools.partial(fused, peers, levels, width // HEADS, fa...  79.5 us
    unnamed x11, local copies, waits for them, and re-layouts  6.08 us

profile of v2, /device:TPU:0, one launch (start us, length us, event | category | flops | bytes accessed | tf_op | source)
XLA Modules:
  0.0 87.6 jit_solution(17211310677405175450)
XLA Ops:
  0.6 1.3 %copy.12.list_ref = s32[8,4]{1,0:T(8,128)} copy(s32[8,4]{0,1:T(4,128)} %bitcast.18) | data formatting | bytes 256 | tf_op jit(solution)/shard_map/squeeze | solution.py:488
  2.0 79.5 %graph_attention.1 = (bf16[256,1024]{1,0:T(8,128)(2,1)}, bf16[256,1024]{1,0:T(8,128)(2,1)}, bf16[256,1024]{1,0:T(8,128)(2,1)}, bf16[256,1024]{1,0:T(8,128)(2,1)}, f32[256,128]{1,0:T(8,128)}) custom-call(s32[8,4]{1,0:T(8,128)} %copy.12.list_ref, s32[8]{0:T(128)} %bitcast.19, bf16[256,1024]{1,0:T(8,128)(2,1)} %bitcast.10, bf16[256,1024]{1,0:T(8,128)(2,1)} %bitcast.11, ...), custom_call_target="tpu_custom_call" | custom-call | tf_op jit(solution)/shard_map/graph_attention/pallas_call | solution.py:450
  81.5 0.0 copy-start.1
  81.5 0.0 copy-start
  81.5 0.0 copy-start.2
  81.5 2.0 %copy.18 = bf16[1,256,1024]{2,1,0:T(8,128)(2,1)} copy(bf16[1,256,1024]{2,1,0:T(8,128)(2,1)} %bitcast.17) | data formatting | bytes 1048576
  83.5 1.9 %copy.19 = bf16[1,256,1024]{2,1,0:T(8,128)(2,1)} copy(bf16[1,256,1024]{2,1,0:T(8,128)(2,1)} %bitcast.16) | data formatting | bytes 1048576
  85.4 0.0 copy-done.1
  85.4 0.8 copy.20
  86.2 0.0 copy-done
  86.2 0.8 copy.21
  86.9 0.0 copy-done.2
  86.9 0.7 copy.22
Async XLA Ops:
  81.5 3.9 %copy-start.1 = (bf16[256,1024]{1,0:T(8,128)(2,1)S(1)}, bf16[256,1024]{1,0:T(8,128)(2,1)}, u32[]{:S(2)}) copy-start(bf16[256,1024]{1,0:T(8,128)(2,1)} %get-tuple-element.12) | copy-start | bytes 1572868
  81.5 4.6 %copy-start = (bf16[256,1024]{1,0:T(8,128)(2,1)S(1)}, bf16[256,1024]{1,0:T(8,128)(2,1)}, u32[]{:S(2)}) copy-start(bf16[256,1024]{1,0:T(8,128)(2,1)} %get-tuple-element.13) | copy-start | bytes 1572868
  81.5 5.4 %copy-start.2 = (f32[256,128]{1,0:T(8,128)S(1)}, f32[256,128]{1,0:T(8,128)}, u32[]{:S(2)}) copy-start(f32[256,128]{1,0:T(8,128)} %get-tuple-element.24) | copy-start | bytes 393220
